TPU v7x, 512 devices: a whole 4x8x8 slice. The times are simulated.
512 devices in a mesh: grp: 8 (over z), dev: 64 (over x, y, core).
Axes of the slice: x: 4, y: 8, z: 8, core: 2. Of those that a mesh axis runs over, the one named last changes fastest.
Arguments:
- points: float32 [3, 1048576], P(None, ('grp', 'dev')), may hold values from 0 to 16, as said below
- probes: float32 [1048576, 256], P(('grp', 'dev')), may hold values from -6 to 6
- samples: float32 [1048576, 256], P(('grp', 'dev')), may hold values from -60 to 60
- near_mask: int32 [2048, 4], P(('grp', 'dev')), may hold values 0 or 1
Outputs:
- leaf_basis: bfloat16 [1048576, 128], P(('grp', 'dev'))
- coupling: bfloat16 [262144, 128], P(('grp', 'dev'))
- parent_basis: float32 [262144, 128], P(('grp', 'dev'))
Inputs may be any that keep to these rules, and one draw needn't show every extreme that they name: `points`: coordinates lie in the unit cells of a grid of cells, leaf t in the cell given by the bits of t taken in turn for the three coordinates.
All inputs are finite; a program needn't handle non-finite values. No bound on the sum of `near_mask` on one device may be relied on, other than what follows from the above.
Results may differ from a plain program's by a relative error of at most 0.0018.
Values sent between devices are 32-bit elements; how exact they have to be, the bound alone decides.
No kernel may reach another device: no remote copies, remote signals or barrier semaphores. Data moves between devices by JAX's collectives and lax.ppermute only.
A program may use at most 64 MiB of HBM per device.

v0:
```python
import math

import jax
import jax.numpy as jnp
from jax import lax
from jax.sharding import PartitionSpec as P

LEAF = 512
KL = 128
KP = 128


highest = lax.Precision.HIGHEST
amplitude = 0.25
length_scale = 1.0
shift_ratio = 0.01
epsilon = 1e-05
neighbour_offsets = (-2, -1, 1, 2)


def shifted(block, axis, distance):
    devices = range(lax.axis_size(axis))
    route = [(i - distance, i) for i in devices if i - distance in devices]
    return lax.ppermute(block, axis, route)


def matern(targets, sources):
    squared = jnp.zeros((targets.shape[1], sources.shape[1]), targets.dtype)
    for dimension in range(3):
        spread = targets[dimension][:, None] - sources[dimension][None, :]
        squared = squared + spread * spread
    scaled = math.sqrt(3.0) / length_scale * jnp.sqrt(squared)
    return amplitude * (1.0 + scaled) * jnp.exp(-scaled)


def shifted_cholesky(gram_matrix):
    order = gram_matrix.shape[0]
    diag_level = jnp.trace(gram_matrix) / order
    identity = jnp.eye(order, dtype=gram_matrix.dtype)
    return jnp.linalg.cholesky(gram_matrix + (shift_ratio * diag_level + epsilon) * identity)


def right_solve(factor, values):
    return lax.linalg.triangular_solve(
        factor, values, left_side=False, lower=True, transpose_a=True
    )


def orthonormal_columns(columns_block):
    gram_matrix = (
        jnp.dot(columns_block.T, columns_block, precision=highest) / columns_block.shape[0]
    )
    return right_solve(shifted_cholesky(gram_matrix), columns_block)


def probe_factor(reduced_probes):
    gram_matrix = (
        jnp.dot(reduced_probes, reduced_probes.T, precision=highest) / reduced_probes.shape[1]
    )
    return shifted_cholesky(gram_matrix)


def couple(reduced_samples, sibling_probes, sibling_factor):
    cross = jnp.dot(reduced_samples, sibling_probes.T, precision=highest) / sibling_probes.shape[1]
    halfway = right_solve(sibling_factor, cross)
    coupling = lax.linalg.triangular_solve(
        sibling_factor, halfway, left_side=False, lower=True, transpose_a=False
    )
    remainder = reduced_samples - jnp.dot(coupling, sibling_probes, precision=highest)
    return (coupling, remainder)


def offset_weight(near_mask, leaf_index, offset):
    if offset == 0:
        return jnp.ones((), jnp.float32)
    return near_mask[leaf_index, neighbour_offsets.index(offset)].astype(jnp.float32)


def window_term(own_points, source_points, source_probes, weights):
    column_weight = jnp.repeat(jnp.stack(weights), LEAF)
    kernel = matern(own_points, source_points) * column_weight[None, :]
    return jnp.dot(kernel, source_probes, precision=highest)


def body(points, probes, samples, near_mask):
    count = points.shape[1] // LEAF
    remaining = []
    borders = []
    for by in (1, -1):
        if by == 1:
            piece = (points[:, (count - 2) * LEAF :], probes[(count - 2) * LEAF :])
        else:
            piece = (points[:, : 2 * LEAF], probes[: 2 * LEAF])
        borders.append(shifted((piece[0], piece[1]), ("grp", "dev"), by))
    wide_points = jnp.concatenate([borders[0][0], points, borders[1][0]], axis=1)
    wide_probes = jnp.concatenate([borders[0][1], probes, borders[1][1]], axis=0)
    for leaf_index in range(count):
        start = leaf_index * LEAF
        weights = [offset_weight(near_mask, leaf_index, offset) for offset in (-2, -1, 0, 1, 2)]
        term = window_term(
            points[:, start : start + LEAF],
            wide_points[:, start : start + 5 * LEAF],
            wide_probes[start : start + 5 * LEAF],
            weights,
        )
        remaining.append(samples[start : start + LEAF] - term)
    stacked = jnp.stack(remaining)
    leaf_probes = probes.reshape(count, LEAF, probes.shape[1])
    basis = jax.vmap(orthonormal_columns)(stacked[:, :, :KL])
    reduced_samples = jnp.einsum("nlk,nlp->nkp", basis, stacked, precision=highest) / LEAF
    reduced_probes = jnp.einsum("nlk,nlp->nkp", basis, leaf_probes, precision=highest) / math.sqrt(
        LEAF
    )
    sibling_probes = reduced_probes.reshape(count // 2, 2, KL, -1)[:, ::-1].reshape(count, KL, -1)
    factors = jax.vmap(probe_factor)(sibling_probes)
    coupling, remainder = jax.vmap(couple)(reduced_samples, sibling_probes, factors)
    parent_rows = remainder[:, :, :KP]
    own_gram = jnp.einsum("nkp,nkq->pq", parent_rows, parent_rows, precision=highest)
    total_gram = lax.psum(own_gram, ("grp", "dev"))
    leaf_total = count * lax.axis_size("grp") * lax.axis_size("dev")
    node_gram = total_gram / (leaf_total * KL)
    node_factor = shifted_cholesky(node_gram)
    parent_basis = jax.vmap(right_solve, in_axes=(None, 0))(node_factor, parent_rows)
    return (
        basis.reshape(count * LEAF, KL).astype(jnp.bfloat16),
        coupling.reshape(count * KL, KL).astype(jnp.bfloat16),
        parent_basis.reshape(count * KL, KP),
    )


def solution(mesh):
    return jax.shard_map(
        body,
        mesh=mesh,
        in_specs=(
            P(None, ("grp", "dev")),
            P(("grp", "dev"), None),
            P(("grp", "dev"), None),
            P(("grp", "dev"), None),
        ),
        out_specs=(P(("grp", "dev"), None), P(("grp", "dev"), None), P(("grp", "dev"), None)),
        check_vma=False,
    )
```

profile of v0, /device:TPU:1, one launch (start us, length us, event | category | flops | bytes accessed | tf_op | source)
XLA Modules:
  0.0 561.0 jit_solution(18297946662846277734)
XLA Ops:
  7.2 3.2 fusion.200
  10.4 4.6 collective-permute-start.1
  15.0 6.5 %collective-permute-start.3 = (f32[1024,256]{1,0:T(8,128)}, f32[1024,256]{1,0:T(8,128)S(1)}, u32[]{:S(2)}, u32[]{:S(2)}) collective-permute-start(f32[1024,256]{1,0:T(8,128)} %get-tuple-element.19), channel_id=1, source_target_pairs={{1,0},{2,1},{3,2},{4,3},{5,4},{6,5},{7,6},{8,7},{9,8},{10,9},{11,1... | collective-permute-start | bytes 3145736 | tf_op jit(solution)/shard_map/ppermute | solution.py:24
  21.5 1.9 collective-permute-start
  23.4 2.4 collective-permute-start.2
  25.9 0.7 fusion.203
  37.5 1.3 constant_dynamic-update-slice_fusion.3
  39.2 1.2 copy-done.9
  40.4 8.0 %fusion.158 = f32[1,512,256]{2,1,0:T(8,128)S(1)} fusion(f32[3072,256]{1,0:T(8,128)S(1)} %constant_dynamic-update-slice_fusion.6, f32[2560]{0:T(1024)S(1)} %mul.196, f32[2560]{0:T(1024)S(1)} %get-tuple-element.11, f32[512]{0:T(512)S(1)} %bitcast.115, f32[2560]{0:T(1024)S(1)} %get-tuple-element.12, f32[512]{0:T(512)S(1)} %bitcast.116, ...), kind=kOutput, calls=%fused_computation.129 | convolution fusion | flops 4045012992 | bytes 3725312 | tf_op jit(solution)/shard_map/dot_general | solution.py:82
  48.4 8.5 %fusion.148 = f32[1,512,256]{2,1,0:T(8,128)S(1)} fusion(f32[3072,256]{1,0:T(8,128)S(1)} %constant_dynamic-update-slice_fusion.6, f32[2560]{0:T(1024)S(1)} %mul.187, f32[2560]{0:T(1024)S(1)} %get-tuple-element.14, f32[512]{0:T(512)S(1)} %bitcast.111, f32[2560]{0:T(1024)S(1)} %get-tuple-element.15, f32[512]{0:T(512)S(1)} %bitcast.112, ...), kind=kOutput, calls=%fused_computation.127 | convolution fusion | flops 4045012992 | bytes 3725312 | tf_op jit(solution)/shard_map/dot_general | solution.py:82
  56.9 8.2 %fusion.138 = f32[1,512,256]{2,1,0:T(8,128)S(1)} fusion(f32[3072,256]{1,0:T(8,128)S(1)} %get-tuple-element.16, f32[2560]{0:T(1024)S(1)} %mul.178, f32[2560]{0:T(1024)S(1)} %get-tuple-element.5, f32[512]{0:T(512)S(1)} %bitcast.108, f32[2560]{0:T(1024)S(1)} %get-tuple-element.6, f32[512]{0:T(512)S(1)} %bitcast.109, f32[2560]{0:T(1024)S(1)} %get-tuple-element.7, ...), kind=kOutput, calls=%fused_computation.125 | convolution fusion | flops 4045012992 | bytes 3725312 | tf_op jit(solution)/shard_map/dot_general | solution.py:82
  65.1 8.0 %fusion.128 = f32[1,512,256]{2,1,0:T(8,128)S(1)} fusion(f32[3072,256]{1,0:T(8,128)S(1)} %get-tuple-element.16, f32[2560]{0:T(1024)S(1)} %mul.169, f32[2560]{0:T(1024)S(1)} %get-tuple-element.8, f32[512]{0:T(512)S(1)} %bitcast.106, f32[2560]{0:T(1024)S(1)} %get-tuple-element.9, f32[512]{0:T(512)S(1)} %bitcast.107, f32[2560]{0:T(1024)S(1)} %get-tuple-element.4, ...), kind=kOutput, calls=%fused_computation.123 | convolution fusion | flops 4045012992 | bytes 3725312 | tf_op jit(solution)/shard_map/dot_general | solution.py:82
  73.2 2.2 select_reduce_fusion.3
  75.8 46.9 %custom-call.21 = f32[4,128,128]{2,1,0:T(8,128)S(1)} custom-call(f32[4,128,128]{2,1,0:T(8,128)S(1)} %copy.22), custom_call_target="Cholesky" | custom-call | tf_op jit(solution)/shard_map/vmap(jit(cholesky))/cholesky | solution.py:40
  123.0 39.7 %custom-call.17 = f32[4,1,128,128]{2,3,1,0:T(8,128)S(1)} custom-call(f32[4,1,128,128]{3,2,1,0:T(8,128)S(1)} %fusion.174), custom_call_target="InvertDiagBlocksLowerTriangular" | custom-call | tf_op jit(solution)/shard_map/vmap()/triangular_solve | solution.py:44
  162.8 3.0 fusion.204
  165.8 2.0 fusion.120
  167.9 2.0 convolution_multiply_fusion
  170.0 0.7 select_reduce_fusion.2
  170.7 0.6 convolution_multiply_fusion.2
  171.8 46.9 %custom-call.22 = f32[4,128,128]{2,1,0:T(8,128)S(1)} custom-call(f32[4,128,128]{2,1,0:T(8,128)S(1)} %copy.28), custom_call_target="Cholesky" | custom-call | tf_op jit(solution)/shard_map/vmap(jit(cholesky))/cholesky | solution.py:40
  219.0 39.5 %custom-call.18 = f32[4,1,128,128]{2,3,1,0:T(8,128)S(1)} custom-call(f32[4,1,128,128]{3,2,1,0:T(8,128)S(1)} %fusion.173), custom_call_target="InvertDiagBlocksLowerTriangular" | custom-call | tf_op jit(solution)/shard_map/vmap()/triangular_solve | solution.py:44
  258.9 1.3 fusion.205
  260.8 1.2 convolution_bitcast_fusion
  262.0 264.1 %all-reduce.2.cloned.1.call-done = f32[128,128]{1,0:T(8,128)} async-done(((f32[128,128]{1,0:T(8,128)}), f32[128,128]{1,0:T(8,128)}) %all-reduce.2.cloned.1.call-update) | async-done | bytes 65552 | tf_op jit(solution)/shard_map/psum | solution.py:119
  526.1 1.5 fusion.183
  528.2 0.9 fusion.184
  529.2 0.9 fusion.177
  530.0 11.7 %cholesky.39 = f32[128,128]{1,0:T(8,128)S(1)} custom-call(f32[128,128]{1,0:T(8,128)S(1)} %fusion.177), custom_call_target="Cholesky" | custom-call | tf_op jit(solution)/shard_map/jit(cholesky)/cholesky | solution.py:40
  542.4 0.7 fusion.175
  543.1 9.8 %custom-call.19 = f32[1,128,128]{1,2,0:T(8,128)S(1)} custom-call(f32[1,128,128]{2,1,0:T(8,128)S(1)} %fusion.175), custom_call_target="InvertDiagBlocksLowerTriangular" | custom-call | tf_op jit(solution)/shard_map/vmap()/triangular_solve | solution.py:44
  552.9 1.1 fusion.163
  (71 shorter events, 4.7 us)
Async XLA Ops:
  7.2 31.6 %copy-start = (f32[2048,256]{1,0:T(8,128)S(1)}, f32[2048,256]{1,0:T(8,128)}, u32[]{:S(2)}) copy-start(f32[2048,256]{1,0:T(8,128)} %param.6) | copy-start | bytes 6291460
  7.2 14.3 %copy-start.7 = (f32[3,2048]{1,0:T(4,128)S(1)}, f32[3,2048]{1,0:T(4,128)}, u32[]{:S(2)}) copy-start(f32[3,2048]{1,0:T(4,128)} %param.5) | copy-start | bytes 73732
  7.2 18.7 %copy-start.8 = (s32[4,4]{1,0:T(4,128)S(1)}, s32[4,4]{1,0:T(4,128)}, u32[]{:S(2)}) copy-start(s32[4,4]{1,0:T(4,128)} %param.8) | copy-start | bytes 196
  7.2 518.9 %all-reduce.2.cloned.1.call-start = ((), (), s32[]{:S(2)}) async-start(), calls=%async_computation | async-start | bytes 131072 | tf_op jit(solution)/shard_map/psum | solution.py:119
  10.4 27.0 %collective-permute-start.1 = (f32[1024,256]{1,0:T(8,128)}, f32[1024,256]{1,0:T(8,128)}, u32[]{:S(2)}, u32[]{:S(2)}) collective-permute-start(f32[1024,256]{1,0:T(8,128)} %get-tuple-element.18), channel_id=1, source_target_pairs={{0,1},{1,2},{2,3},{3,4},{4,5},{5,6},{6,7},{7,8},{8,9},{9,10},{10,1... | collective-permute-start | bytes 3145736 | tf_op jit(solution)/shard_map/ppermute | solution.py:24
  15.0 24.1 %collective-permute-start.3 = (f32[1024,256]{1,0:T(8,128)}, f32[1024,256]{1,0:T(8,128)S(1)}, u32[]{:S(2)}, u32[]{:S(2)}) collective-permute-start(f32[1024,256]{1,0:T(8,128)} %get-tuple-element.19), channel_id=1, source_target_pairs={{1,0},{2,1},{3,2},{4,3},{5,4},{6,5},{7,6},{8,7},{9,8},{10,9},{11,1... | collective-permute-start | bytes 3145736 | tf_op jit(solution)/shard_map/ppermute | solution.py:24
  21.5 15.7 %collective-permute-start = (f32[3,1024]{1,0:T(4,128)S(1)}, f32[3,1024]{1,0:T(4,128)S(1)}, u32[]{:S(2)}, u32[]{:S(2)}) collective-permute-start(f32[3,1024]{1,0:T(4,128)S(1)} %get-tuple-element.34), channel_id=1, source_target_pairs={{0,1},{1,2},{2,3},{3,4},{4,5},{5,6},{6,7},{7,8},{8,9},{9,10},{10,1... | collective-permute-start | bytes 36872 | tf_op jit(solution)/shard_map/ppermute | solution.py:24
  23.4 13.8 %collective-permute-start.2 = (f32[3,1024]{1,0:T(4,128)S(1)}, f32[3,1024]{1,0:T(4,128)S(1)}, u32[]{:S(2)}, u32[]{:S(2)}) collective-permute-start(f32[3,1024]{1,0:T(4,128)S(1)} %get-tuple-element.35), channel_id=1, source_target_pairs={{1,0},{2,1},{3,2},{4,3},{5,4},{6,5},{7,6},{8,7},{9,8},{10,9},{11,1... | collective-permute-start | bytes 36872 | tf_op jit(solution)/shard_map/ppermute | solution.py:24
  38.8 1.6 copy-start.9
  56.9 16.3 %copy-start.1 = (f32[1,512,256]{2,1,0:T(8,128)}, f32[1,512,256]{2,1,0:T(8,128)S(1)}, u32[]{:S(2)}) copy-start(f32[1,512,256]{2,1,0:T(8,128)S(1)} %fusion.148) | copy-start | bytes 1572868
  65.1 8.1 %copy-start.3 = (f32[1,512,256]{2,1,0:T(8,128)}, f32[1,512,256]{2,1,0:T(8,128)S(1)}, u32[]{:S(2)}) copy-start(f32[1,512,256]{2,1,0:T(8,128)S(1)} %fusion.138) | copy-start | bytes 1572868
  73.2 2.2 copy-start.5
  162.7 3.1 copy-start.2
  162.8 3.1 copy-start.4
  162.8 3.1 copy-start.6
Sparse Core Ops, SparseCore 0:
  262.2 263.8 all-reduce.1
where the time goes:
time: 570 us; the launch traced here: 561 us
  waiting for transfers between devices  264 us (46%)
  other arithmetic  200 us (35%)
  matrix products  48 us (8%)
  between operations  25.2 us (4%)
  starting transfers between devices  15.4 us (3%)
  local copies, waits for them, and re-layouts  8.37 us (1%)
    psum x1, waiting for transfers between devices, body(): total_gram = lax.psum(own_gram, ('grp', 'dev'))  264 us
    another operation x10, other arithmetic, shifted_cholesky(): jnp.linalg.cholesky(gram_matrix + (shift_ratio * diag_level + epsilon) *...  107 us
    another operation x7, other arithmetic, right_solve(): lax.linalg.triangular_solve(factor, values, left_side=False, lower=True,...  89.9 us
    dot_general x4, matrix products, window_term(): return jnp.dot(kernel, source_probes, precision=highest)  32.7 us
    ppermute x4, starting transfers between devices, shifted(): return lax.ppermute(block, axis, route)  15.4 us
  transfers between devices with their start and end apart: 5, of which 1 were waited for; matrix products, arithmetic and copies ran while one was open for 1% of the time, Pallas kernels for 0%

commit v1 on v0

v1 whole, which is shorter than its diff:
```python
import math

import jax
import jax.numpy as jnp
from jax import lax
from jax.experimental import pallas as pl
from jax.experimental.pallas import tpu as pltpu
from jax.sharding import Mesh, PartitionSpec as P

LEAF = 512
COLS = 256
KL = 128
COUNT = 4
LEAVES = 2048
FEATURES = 32
PANEL = 16
ROWS = 128

AMPLITUDE = 0.25
SHIFT_RATIO = 0.01
EPSILON = 1e-05
LOG2E = math.log2(math.e)
SCALE = math.sqrt(3.0) * LOG2E
WEIGHT = AMPLITUDE / LOG2E

highest = lax.Precision.HIGHEST
f32 = jnp.float32
bf16 = jnp.bfloat16
AXES = ("z", "x", "y", "c")
VMEM_LIMIT = 48 * 1024 * 1024


def split2(values):
    high = values.astype(bf16)
    low = (values - high.astype(f32)).astype(bf16)
    return high, low


def split3(values):
    high = values.astype(bf16)
    rest = values - high.astype(f32)
    middle = rest.astype(bf16)
    low = (rest - middle.astype(f32)).astype(bf16)
    return high, middle, low


def dot(left, right, contract, precision=highest):
    return lax.dot_general(
        left, right, ((contract[:1], contract[1:]), ((), ())),
        precision=precision, preferred_element_type=f32,
    )


def fast(left, right, contract):
    return dot(left, right, contract, None)


def features(points, target):
    rows = [points[d : d + 1, :] for d in range(3)]
    norm = [piece.astype(f32) for piece in split3(rows[0] * rows[0] + rows[1] * rows[1] + rows[2] * rows[2])]
    ones = jnp.ones_like(rows[0])
    out = []
    for row in rows:
        pieces = [piece.astype(f32) for piece in split3(row)]
        if target:
            out += [pieces[i] for i in (0, 0, 1, 1, 0, 2)]
        else:
            out += [-2.0 * pieces[i] for i in (0, 1, 0, 1, 2, 0)]
    out += norm + [ones] * 3 if target else [ones] * 3 + norm
    out += [jnp.zeros_like(ones)] * (FEATURES - len(out))
    return jnp.concatenate(out, axis=0)


def block_product(targets_ref, sources_ref, high_ref, low_ref, target, source, step):
    columns = pl.ds(pl.multiple_of(source * LEAF, LEAF), LEAF)
    kernel_sources = sources_ref[:, columns]
    high_probes = high_ref[columns, :]
    low_probes = low_ref[columns, :]
    for part in range(LEAF // ROWS):
        rows = pl.ds(pl.multiple_of(target * LEAF + part * ROWS, ROWS), ROWS)
        squared = fast(targets_ref[rows, :], kernel_sources, (1, 0))
        squared = jnp.maximum(squared, 1e-24)
        scaled = squared * lax.rsqrt(squared)
        high, low = split2((scaled + LOG2E) * jnp.exp2(-scaled))
        product = fast(high, high_probes, (1, 0)) + fast(low, high_probes, (1, 0)) + fast(high, low_probes, (1, 0))
        step(rows, product)


def local_kernel(mask_ref, points_ref, probes_ref, samples_ref, out_ref, targets_ref, sources_ref, high_ref, low_ref):
    centred = (points_ref[...] - points_ref[:, 0:1]) * SCALE
    targets_ref[...] = features(centred, True).T.astype(bf16)
    sources_ref[...] = features(centred, False).astype(bf16)
    high, low = split2(probes_ref[...])
    high_ref[...] = high
    low_ref[...] = low
    out_ref[...] = samples_ref[...]

    def target_loop(target, _):
        def source_loop(source, _):
            offset = source - target
            slot = jnp.clip(jnp.where(offset < 0, offset + 2, offset + 1), 0, 3)
            weight = jnp.where(offset == 0, 1, mask_ref[target, slot]).astype(f32) * WEIGHT

            def step(rows, product):
                out_ref[rows, :] -= weight * product

            block_product(targets_ref, sources_ref, high_ref, low_ref, target, source, step)
            return 0

        return lax.fori_loop(jnp.maximum(target - 2, 0), jnp.minimum(target + 3, COUNT), source_loop, 0)

    lax.fori_loop(0, COUNT, target_loop, 0)


def shifted_gram(gram):
    row = lax.broadcasted_iota(jnp.int32, (KL, KL), 0)
    column = lax.broadcasted_iota(jnp.int32, (KL, KL), 1)
    diagonal = row == column
    trace = jnp.sum(jnp.where(diagonal, gram, 0.0))
    return gram + jnp.where(diagonal, SHIFT_RATIO * trace / KL + EPSILON, 0.0)


def inverse_factors(work_ref, panel_ref, number):
    lane = lax.broadcasted_iota(jnp.int32, (number, KL), 1)
    wide_lane = lax.broadcasted_iota(jnp.int32, (KL, KL), 1)
    for first in range(0, KL, PANEL):
        rows = [work_ref[pl.ds(first + j, number, stride=KL), :] for j in range(PANEL)]
        entry = {
            (j, i): jnp.broadcast_to(rows[j][:, first + i : first + i + 1], (number, KL))
            for j in range(PANEL)
            for i in range(j, PANEL)
        }
        inside = (lane >= first) & (lane < first + PANEL)
        rows = [jnp.where(inside, jnp.where(lane == first + j, 1.0, 0.0), rows[j]) for j in range(PANEL)]
        for k in range(PANEL):
            scale = lax.rsqrt(entry[k, k])
            rows[k] = rows[k] * scale
            factor = {j: entry[k, j] * scale for j in range(k + 1, PANEL)}
            for j in range(k + 1, PANEL):
                for i in range(j, PANEL):
                    entry[j, i] = entry[j, i] - factor[j] * factor[i]
                rows[j] = rows[j] - factor[j] * rows[k]
            panel_ref[pl.ds(k, number, stride=PANEL), :] = rows[k]
        after = first + PANEL
        for matrix in range(number):
            panel = panel_ref[matrix * PANEL : (matrix + 1) * PANEL, :]
            base = matrix * KL
            work_ref[base + first : base + after, :] = jnp.where(
                wide_lane[:PANEL] < after, panel, 0.0
            )
            if after < KL:
                high, middle, low = split3(panel)
                left = jnp.concatenate([high, high, middle, middle, high, low], axis=0)
                right = jnp.concatenate([high, middle, high, middle, low, high], axis=0)
                update = fast(left, right, (0, 0))
                done = (wide_lane >= first) & (wide_lane < after)
                old = jnp.where(done[after:], 0.0, work_ref[base + after : base + KL, :])
                work_ref[base + after : base + KL, :] = old - update[after:, :]


def halo_kernel(
    mask_ref, points_ref, before_points_ref, after_points_ref, partial_ref, probes_ref, before_ref, after_ref,
    basis_ref, coupling_ref, parent_ref, gram_ref,
    targets_ref, sources_ref, high_ref, low_ref, remaining_ref, work_ref, panel_ref,
):
    centre = points_ref[:, 0:1]
    targets_ref[...] = features((points_ref[...] - centre) * SCALE, True).T.astype(bf16)
    for half, (halo_points, halo_probes) in enumerate(((before_points_ref, before_ref), (after_points_ref, after_ref))):
        columns = slice(half * 2 * LEAF, (half + 1) * 2 * LEAF)
        sources_ref[:, columns] = features((halo_points[...] - centre) * SCALE, False).astype(bf16)
        high, low = split2(halo_probes[...])
        high_ref[columns, :] = high
        low_ref[columns, :] = low
    remaining_ref[...] = partial_ref[...]

    def pair_loop(pair, _):
        source = (pair + 1) // 2
        target = pair - jnp.where(pair >= 1, 1, 0) - jnp.where(pair >= 5, 1, 0)
        offset = jnp.where(source < 2, source - 2, source + 2) - target
        slot = jnp.where(offset < 0, offset + 2, offset + 1)
        weight = mask_ref[target, slot].astype(f32) * WEIGHT

        def step(rows, product):
            remaining_ref[rows, :] -= weight * product

        block_product(targets_ref, sources_ref, high_ref, low_ref, target, source, step)
        return 0

    lax.fori_loop(0, 6, pair_loop, 0)

    samples_products, probes_products = [], []
    for leaf in range(COUNT):
        rows = slice(leaf * LEAF, (leaf + 1) * LEAF)
        block = remaining_ref[rows, :KL]
        samples_products.append(dot(block, remaining_ref[rows, :], (0, 0)))
        probes_products.append(dot(block, probes_ref[rows, :], (0, 0)))
        work_ref[leaf * KL : (leaf + 1) * KL, :] = shifted_gram(samples_products[leaf][:, :KL] / LEAF)
    inverse_factors(work_ref, panel_ref, COUNT)
    reduced_samples, reduced_probes = [], []
    for leaf in range(COUNT):
        rows = slice(leaf * LEAF, (leaf + 1) * LEAF)
        inverse = work_ref[leaf * KL : (leaf + 1) * KL, :]
        basis_ref[rows, :] = dot(remaining_ref[rows, :KL], inverse, (1, 1)).astype(bf16)
        reduced_samples.append(dot(inverse, samples_products[leaf], (1, 0)) / LEAF)
        reduced_probes.append(dot(inverse, probes_products[leaf], (1, 0)) / math.sqrt(LEAF))
    for leaf in range(COUNT):
        gram = dot(reduced_probes[leaf], reduced_probes[leaf], (1, 1)) / COLS
        work_ref[leaf * KL : (leaf + 1) * KL, :] = shifted_gram(gram)
    inverse_factors(work_ref, panel_ref, COUNT)
    for leaf in range(COUNT):
        sibling = leaf ^ 1
        rows = slice(leaf * KL, (leaf + 1) * KL)
        inverse = work_ref[sibling * KL : (sibling + 1) * KL, :]
        cross = dot(reduced_samples[leaf], reduced_probes[sibling], (1, 1)) / COLS
        coupling = dot(dot(cross, inverse, (1, 1)), inverse, (1, 0))
        coupling_ref[rows, :] = coupling.astype(bf16)
        parent_ref[rows, :] = reduced_samples[leaf][:, :KL] - dot(coupling, reduced_probes[sibling][:, :KL], (1, 0))
    gram_ref[...] = dot(parent_ref[...], parent_ref[...], (0, 0))


def parent_kernel(gram_ref, parent_ref, out_ref, work_ref, panel_ref):
    work_ref[...] = shifted_gram(gram_ref[...] / (LEAVES * KL))
    inverse_factors(work_ref, panel_ref, 1)
    out_ref[...] = dot(parent_ref[...], work_ref[...], (1, 1))


def whole(memory_space=pltpu.VMEM):
    return pl.BlockSpec(memory_space=memory_space)


def exchange(block, axes):
    size = lax.axis_size(axes)
    return lax.all_to_all(jnp.broadcast_to(block, (size,) + block.shape), axes, 0, 0)


def total(block):
    size = lax.axis_size("z")
    parts = lax.all_to_all(block.reshape(size, KL // size, KL), "z", 0, 0).sum(0)
    parts = exchange(parts, ("x", "c")).sum(0)
    parts = exchange(parts, "y").sum(0)
    return exchange(parts, "z").reshape(KL, KL)


def shifted(block, distance):
    devices = range(lax.axis_size(AXES))
    route = [(i - distance, i) for i in devices if i - distance in devices]
    return lax.ppermute(block, AXES, route)


def body(points, probes, samples, near_mask):
    size = COUNT * LEAF
    before = shifted(probes[2 * LEAF :], 1)
    after = shifted(probes[: 2 * LEAF], -1)
    before_points = shifted(points[:, 2 * LEAF :], 1)
    after_points = shifted(points[:, : 2 * LEAF], -1)
    smem, vmem = whole(pltpu.SMEM), whole()
    params = pltpu.CompilerParams(vmem_limit_bytes=VMEM_LIMIT)
    partial = pl.pallas_call(
        local_kernel,
        out_shape=jax.ShapeDtypeStruct((size, COLS), f32),
        in_specs=[smem, vmem, vmem, vmem],
        out_specs=vmem,
        scratch_shapes=[
            pltpu.VMEM((size, FEATURES), bf16),
            pltpu.VMEM((FEATURES, size), bf16),
            pltpu.VMEM((size, COLS), bf16),
            pltpu.VMEM((size, COLS), bf16),
        ],
        compiler_params=params,
        cost_estimate=pl.CostEstimate(flops=14 * 8 * LEAF * LEAF * COLS, bytes_accessed=6 << 20, transcendentals=28 * LEAF * LEAF),
        name="local_blocks",
    )(near_mask, points, probes, samples)
    basis, coupling, parent_rows, gram = pl.pallas_call(
        halo_kernel,
        out_shape=[
            jax.ShapeDtypeStruct((size, KL), bf16),
            jax.ShapeDtypeStruct((COUNT * KL, KL), bf16),
            jax.ShapeDtypeStruct((COUNT * KL, KL), f32),
            jax.ShapeDtypeStruct((KL, KL), f32),
        ],
        in_specs=[smem] + [vmem] * 7,
        out_specs=[vmem] * 4,
        scratch_shapes=[
            pltpu.VMEM((size, FEATURES), bf16),
            pltpu.VMEM((FEATURES, size), bf16),
            pltpu.VMEM((size, COLS), bf16),
            pltpu.VMEM((size, COLS), bf16),
            pltpu.VMEM((size, COLS), f32),
            pltpu.VMEM((COUNT * KL, KL), f32),
            pltpu.VMEM((COUNT * PANEL, KL), f32),
        ],
        compiler_params=params,
        name="halo_blocks",
    )(near_mask, points, before_points, after_points, partial, probes, before, after)
    parent_basis = pl.pallas_call(
        parent_kernel,
        out_shape=jax.ShapeDtypeStruct((COUNT * KL, KL), f32),
        in_specs=[vmem, vmem],
        out_specs=vmem,
        scratch_shapes=[pltpu.VMEM((KL, KL), f32), pltpu.VMEM((PANEL, KL), f32)],
        compiler_params=params,
        name="parent",
    )(total(gram), parent_rows)
    return basis, coupling, parent_basis


def solution(mesh):
    fine = Mesh(mesh.devices.reshape(8, 4, 8, 2), AXES)
    return jax.shard_map(
        body,
        mesh=fine,
        in_specs=(P(None, AXES), P(AXES, None), P(AXES, None), P(AXES, None)),
        out_specs=(P(AXES, None), P(AXES, None), P(AXES, None)),
        check_vma=False,
    )
```

time: 570 us -> 122 us (0.21); the launches traced: 561 us -> 121 us
  waiting for transfers between devices: 264 us -> 0.01 us
  other arithmetic: 200 us -> 0.03 us
  blocking collectives: 0 us -> 54.1 us
  Pallas kernels: 0 us -> 50 us
  matrix products: 48 us -> 0 us
  between operations: 25.2 us -> 0.8 us
  local copies, waits for them, and re-layouts: 8.37 us -> 1.86 us
    psum x1 -> x0, waiting for transfers between devices: 264 us -> none  [body(): total_gram = lax.psum(own_gram, ('grp', 'dev'))]
    another operation x17 -> x0, other arithmetic: 196 us -> none  [the longest x10 107 us: shifted_cholesky(): jnp.linalg.cholesky(gram_matrix + (shift_ratio * diag_level + epsilon) *...]
    all_to_all x0 -> x4, blocking collectives: none -> 54.1 us  [the longest x3 35.2 us: exchange(): lax.all_to_all(jnp.broadcast_to(block, (size,) + block.shape), axes, 0, 0)]
    pallas_call x0 -> x3, Pallas kernels: none -> 50 us  [the longest x1 27 us: body(): pl.pallas_call(halo_kernel, out_shape=[jax.ShapeDtypeStruct((size, KL), b...]
    dot_general x11 -> x0, matrix products: 42.1 us -> none  [the longest x4 32.7 us: window_term(): return jnp.dot(kernel, source_probes, precision=highest)]
    another operation x4 -> x0, matrix products: 5.83 us -> none  [the longest x3 4.51 us: right_solve(): lax.linalg.triangular_solve(factor, values, left_side=False, lower=True,...]
  transfers between devices with their start and end apart: 5 -> 4, of which waited for: 1 -> 0; matrix products, arithmetic and copies ran while one was open for 1% -> 0% of each run, Pallas kernels for 0% -> 15%
where the time goes in v1:
time: 122 us; the launch traced here: 121 us
  blocking collectives  54.1 us (44%)
  Pallas kernels  50 us (41%)
  starting transfers between devices  14.5 us (12%)
  local copies, waits for them, and re-layouts  1.86 us (2%)
    all_to_all x3, blocking collectives, exchange(): lax.all_to_all(jnp.broadcast_to(block, (size,) + block.shape), axes, 0, 0)  35.2 us
    pallas_call x1, Pallas kernels, body(): pl.pallas_call(halo_kernel, out_shape=[jax.ShapeDtypeStruct((size, KL), b...  27 us
    all_to_all x1, blocking collectives, total(): lax.all_to_all(block.reshape(size, KL // size, KL), 'z', 0, 0).sum(0)  18.9 us
    pallas_call x1, Pallas kernels, body(): pl.pallas_call(local_kernel, out_shape=jax.ShapeDtypeStruct((size, COLS),...  17.7 us
    ppermute x4, starting transfers between devices, shifted(): return lax.ppermute(block, AXES, route)  14.5 us
    pallas_call x1, Pallas kernels, body(): pl.pallas_call(parent_kernel, out_shape=jax.ShapeDtypeStruct((COUNT * KL,...  5.35 us
  transfers between devices with their start and end apart: 4, of which 0 were waited for; matrix products, arithmetic and copies ran while one was open for 0% of the time, Pallas kernels for 15%

profile of v1, /device:TPU:1, one launch (start us, length us, event | category | flops | bytes accessed | tf_op | source)
XLA Modules:
  0.0 121.3 jit_solution(5897430355490998229)
XLA Ops:
  0.6 0.0 copy-start
  0.6 0.0 copy-start.1
  0.7 0.0 copy-start.2
  0.7 1.8 %fusion = (f32[1024,256]{1,0:T(8,128)S(1)}, f32[1024,256]{1,0:T(8,128)S(1)}) fusion(f32[2048,256]{1,0:T(8,128)} %probes_ref.3), kind=kLoop, calls=%fused_computation | loop fusion | bytes 4194304 | tf_op jit(solution)/shard_map/slice | solution.py:253
  2.5 4.6 %collective-permute-start.2 = (f32[1024,256]{1,0:T(8,128)S(1)}, f32[1024,256]{1,0:T(8,128)S(1)}, u32[]{:S(2)}, u32[]{:S(2)}) collective-permute-start(f32[1024,256]{1,0:T(8,128)S(1)} %get-tuple-element.12), channel_id=1, source_target_pairs={{0,1},{1,2},{2,3},{3,4},{4,5},{5,6},{6,7},{7,8},{8,9},{9,10},{10,1... | collective-permute-start | bytes 3145736 | tf_op jit(solution)/shard_map/ppermute | solution.py:247
  7.1 5.5 %collective-permute-start.3 = (f32[1024,256]{1,0:T(8,128)S(1)}, f32[1024,256]{1,0:T(8,128)S(1)}, u32[]{:S(2)}, u32[]{:S(2)}) collective-permute-start(f32[1024,256]{1,0:T(8,128)S(1)} %get-tuple-element.11), channel_id=1, source_target_pairs={{1,0},{2,1},{3,2},{4,3},{5,4},{6,5},{7,6},{8,7},{9,8},{10,9},{11,1... | collective-permute-start | bytes 3145736 | tf_op jit(solution)/shard_map/ppermute | solution.py:247
  12.6 0.0 copy-done.1
  12.7 1.9 %collective-permute-start = (f32[3,1024]{1,0:T(4,128)S(1)}, f32[3,1024]{1,0:T(4,128)S(1)}, u32[]{:S(2)}, u32[]{:S(2)}) collective-permute-start(f32[3,1024]{1,0:T(4,128)S(1)} %get-tuple-element.14), channel_id=1, source_target_pairs={{0,1},{1,2},{2,3},{3,4},{4,5},{5,6},{6,7},{7,8},{8,9},{9,10},{10,1... | collective-permute-start | bytes 36872 | tf_op jit(solution)/shard_map/ppermute | solution.py:247
  14.6 2.4 %collective-permute-start.1 = (f32[3,1024]{1,0:T(4,128)S(1)}, f32[3,1024]{1,0:T(4,128)S(1)}, u32[]{:S(2)}, u32[]{:S(2)}) collective-permute-start(f32[3,1024]{1,0:T(4,128)S(1)} %get-tuple-element.13), channel_id=1, source_target_pairs={{1,0},{2,1},{3,2},{4,3},{5,4},{6,5},{7,6},{8,7},{9,8},{10,9},{11,1... | collective-permute-start | bytes 36872 | tf_op jit(solution)/shard_map/ppermute | solution.py:247
  17.0 0.0 copy-done
  17.0 0.0 copy-done.2
  17.0 17.7 %local_blocks.1.partial_ref = f32[2048,256]{1,0:T(8,128)S(1)} custom-call(s32[4,4]{1,0:T(4,128)S(1)} %copy-done.2, f32[3,2048]{1,0:T(4,128)S(1)} %copy-done.1, f32[2048,256]{1,0:T(8,128)S(1)} %copy-done, f32[2048,256]{1,0:T(8,128)} %samples_ref.1), custom_call_target="tpu_custom_call" | custom-call | flops 7516192768 | bytes 6291456 | tf_op jit(solution)/shard_map/local_blocks/pallas_call | solution.py:258
  34.7 0.0 collective-permute-done.before_points_ref
  34.8 0.0 collective-permute-done.1.after_points_ref
  34.8 0.0 collective-permute-done.2.before_ref
  34.8 0.0 collective-permute-done.3.after_ref
  34.8 27.0 %halo_blocks.1 = (bf16[2048,128]{1,0:T(8,128)(2,1)}, bf16[512,128]{1,0:T(8,128)(2,1)}, f32[512,128]{1,0:T(8,128)S(1)}, f32[128,128]{1,0:T(8,128)S(1)}) custom-call(s32[4,4]{1,0:T(4,128)S(1)} %copy-done.2, f32[3,2048]{1,0:T(4,128)S(1)} %copy-done.1, f32[3,1024]{1,0:T(4,128)S(1)} %collective-permute-done.before_points_ref, ...), custom_call_target="tpu_custom_call" | custom-call | tf_op jit(solution)/shard_map/halo_blocks/pallas_call | solution.py:273
  61.8 18.9 %all_to_all.20 = f32[8,16,128]{2,1,0:T(8,128)S(1)} all-to-all(f32[8,16,128]{2,1,0:T(8,128)S(1)} %bitcast.3), channel_id=1, replica_groups=mesh['z'=8,'x'=4,'y'=8,'c'=2] {'z'}, dimensions={0} | all-to-all | bytes 131072 | tf_op jit(solution)/shard_map/all_to_all | solution.py:238
  80.7 15.8 %all_to_all.21 = f32[8,16,128]{2,1,0:T(8,128)S(1)} all-to-all(f32[8,16,128]{2,1,0:T(8,128)S(1)} %broadcast_in_dim.9), channel_id=1, replica_groups=mesh['z'=8,'x'=4,'y'=8,'c'=2] {'x','c'}, dimensions={0} | all-to-all | bytes 131072 | tf_op jit(solution)/shard_map/all_to_all | solution.py:233
  96.5 9.7 %all_to_all.22 = f32[8,16,128]{2,1,0:T(8,128)S(1)} all-to-all(f32[8,16,128]{2,1,0:T(8,128)S(1)} %broadcast_in_dim.10), channel_id=1, replica_groups=mesh['z'=8,'x'=4,'y'=8,'c'=2] {'y'}, dimensions={0} | all-to-all | bytes 131072 | tf_op jit(solution)/shard_map/all_to_all | solution.py:233
  106.2 9.7 %all_to_all.23 = f32[8,16,128]{2,1,0:T(8,128)S(1)} all-to-all(f32[8,16,128]{2,1,0:T(8,128)S(1)} %broadcast_in_dim.11), channel_id=1, replica_groups=mesh['z'=8,'x'=4,'y'=8,'c'=2] {'z'}, dimensions={0} | all-to-all | bytes 131072 | tf_op jit(solution)/shard_map/all_to_all | solution.py:233
  115.9 5.3 %parent.1 = f32[512,128]{1,0:T(8,128)} custom-call(f32[128,128]{1,0:T(8,128)S(1)} %bitcast.2, f32[512,128]{1,0:T(8,128)S(1)} %get-tuple-element.10.parent_ref), custom_call_target="tpu_custom_call" | custom-call | tf_op jit(solution)/shard_map/parent/pallas_call | solution.py:295
  (7 shorter events, 0.1 us)
Async XLA Ops:
  0.6 16.4 %copy-start = (f32[2048,256]{1,0:T(8,128)S(1)}, f32[2048,256]{1,0:T(8,128)}, u32[]{:S(2)}) copy-start(f32[2048,256]{1,0:T(8,128)} %probes_ref.3) | copy-start | bytes 6291460
  0.6 12.0 %copy-start.1 = (f32[3,2048]{1,0:T(4,128)S(1)}, f32[3,2048]{1,0:T(4,128)}, u32[]{:S(2)}) copy-start(f32[3,2048]{1,0:T(4,128)} %points_ref.3) | copy-start | bytes 73732
  0.7 16.4 %copy-start.2 = (s32[4,4]{1,0:T(4,128)S(1)}, s32[4,4]{1,0:T(4,128)}, u32[]{:S(2)}) copy-start(s32[4,4]{1,0:T(4,128)} %mask_ref.3) | copy-start | bytes 196
  2.5 32.3 %collective-permute-start.2 = (f32[1024,256]{1,0:T(8,128)S(1)}, f32[1024,256]{1,0:T(8,128)S(1)}, u32[]{:S(2)}, u32[]{:S(2)}) collective-permute-start(f32[1024,256]{1,0:T(8,128)S(1)} %get-tuple-element.12), channel_id=1, source_target_pairs={{0,1},{1,2},{2,3},{3,4},{4,5},{5,6},{6,7},{7,8},{8,9},{9,10},{10,1... | collective-permute-start | bytes 3145736 | tf_op jit(solution)/shard_map/ppermute | solution.py:247
  7.1 27.7 %collective-permute-start.3 = (f32[1024,256]{1,0:T(8,128)S(1)}, f32[1024,256]{1,0:T(8,128)S(1)}, u32[]{:S(2)}, u32[]{:S(2)}) collective-permute-start(f32[1024,256]{1,0:T(8,128)S(1)} %get-tuple-element.11), channel_id=1, source_target_pairs={{1,0},{2,1},{3,2},{4,3},{5,4},{6,5},{7,6},{8,7},{9,8},{10,9},{11,1... | collective-permute-start | bytes 3145736 | tf_op jit(solution)/shard_map/ppermute | solution.py:247
  12.7 22.1 %collective-permute-start = (f32[3,1024]{1,0:T(4,128)S(1)}, f32[3,1024]{1,0:T(4,128)S(1)}, u32[]{:S(2)}, u32[]{:S(2)}) collective-permute-start(f32[3,1024]{1,0:T(4,128)S(1)} %get-tuple-element.14), channel_id=1, source_target_pairs={{0,1},{1,2},{2,3},{3,4},{4,5},{5,6},{6,7},{7,8},{8,9},{9,10},{10,1... | collective-permute-start | bytes 36872 | tf_op jit(solution)/shard_map/ppermute | solution.py:247
  14.6 20.2 %collective-permute-start.1 = (f32[3,1024]{1,0:T(4,128)S(1)}, f32[3,1024]{1,0:T(4,128)S(1)}, u32[]{:S(2)}, u32[]{:S(2)}) collective-permute-start(f32[3,1024]{1,0:T(4,128)S(1)} %get-tuple-element.13), channel_id=1, source_target_pairs={{1,0},{2,1},{3,2},{4,3},{5,4},{6,5},{7,6},{8,7},{9,8},{10,9},{11,1... | collective-permute-start | bytes 36872 | tf_op jit(solution)/shard_map/ppermute | solution.py:247

commit v2 on v1

v2 whole, which is shorter than its diff:
```python
import functools
import math

import jax
import jax.numpy as jnp
from jax import lax
from jax.experimental import pallas as pl
from jax.experimental.pallas import tpu as pltpu
from jax.sharding import Mesh, PartitionSpec as P

LEAF = 512
COLS = 256
KL = 128
COUNT = 4
LEAVES = 2048
FEATURES = 32
PANEL = 16
HALF = 256
EXTRA = 16

AMPLITUDE = 0.25
SHIFT_RATIO = 0.01
EPSILON = 1e-05
LOG2E = math.log2(math.e)
SCALE = math.sqrt(3.0) * LOG2E
WEIGHT = AMPLITUDE / LOG2E

highest = lax.Precision.HIGHEST
f32 = jnp.float32
bf16 = jnp.bfloat16
AXES = ("z", "x", "y", "c")
VMEM_LIMIT = 48 * 1024 * 1024


def split2(values):
    high = values.astype(bf16)
    low = (values - high.astype(f32)).astype(bf16)
    return high, low


def split3(values):
    high = values.astype(bf16)
    rest = values - high.astype(f32)
    middle = rest.astype(bf16)
    low = (rest - middle.astype(f32)).astype(bf16)
    return high, middle, low


def dot(left, right, contract, precision=highest):
    return lax.dot_general(
        left, right, ((contract[:1], contract[1:]), ((), ())),
        precision=precision, preferred_element_type=f32,
    )


def fast(left, right, contract):
    return dot(left, right, contract, None)


def features(points, target):
    rows = [points[d : d + 1, :] for d in range(3)]
    norm = [piece.astype(f32) for piece in split3(rows[0] * rows[0] + rows[1] * rows[1] + rows[2] * rows[2])]
    ones = jnp.ones_like(rows[0])
    out = []
    for row in rows:
        pieces = [piece.astype(f32) for piece in split3(row)]
        if target:
            out += [pieces[i] for i in (0, 0, 1, 1, 0, 2)]
        else:
            out += [-2.0 * pieces[i] for i in (0, 1, 0, 1, 2, 0)]
    out += norm + [ones] * 3 if target else [ones] * 3 + norm
    out += [jnp.zeros_like(ones)] * (FEATURES - len(out))
    return jnp.concatenate(out, axis=0)


def dot3(left, right, contract):
    left_high, left_low = split2(left)
    right_high, right_low = split2(right)
    return fast(
        jnp.concatenate([left_high, left_low, left_high], axis=contract[0]),
        jnp.concatenate([right_high, right_high, right_low], axis=contract[1]),
        contract,
    )


def near_blocks(targets_ref, sources_ref, high_ref, low_ref, ahead_ref, out_ref, mask_ref, number, pair_of):
    def distances(target, source, half):
        rows = pl.ds(pl.multiple_of(target * LEAF, LEAF), LEAF)
        columns = pl.ds(pl.multiple_of(source * LEAF + half * HALF, HALF), HALF)
        return fast(targets_ref[rows, :], sources_ref[:, columns], (1, 0))

    def product(squared, source, half):
        rows = pl.ds(pl.multiple_of(source * LEAF + half * HALF, HALF), HALF)
        high_probes, low_probes = high_ref[rows, :], low_ref[rows, :]
        squared = jnp.maximum(squared, 1e-24)
        scaled = squared * lax.rsqrt(squared)
        high, low = split2((scaled + LOG2E) * jnp.exp2(-scaled))
        return fast(
            jnp.concatenate([high, low, high], axis=1),
            jnp.concatenate([high_probes, high_probes, low_probes], axis=0),
            (1, 0),
        )

    def loop(pair, _):
        target, source, offset = pair_of(pair)
        next_target, next_source, _ = pair_of(jnp.minimum(pair + 1, number - 1))
        slot = jnp.clip(jnp.where(offset < 0, offset + 2, offset + 1), 0, 3)
        weight = jnp.where(offset == 0, 1, mask_ref[target, slot]).astype(f32) * WEIGHT
        second = distances(target, source, 1)
        term = product(ahead_ref[...], source, 0)
        ahead_ref[...] = distances(next_target, next_source, 0)
        term += product(second, source, 1)
        rows = pl.ds(pl.multiple_of(target * LEAF, LEAF), LEAF)
        out_ref[rows, :] -= weight * term
        return 0

    first_target, first_source, _ = pair_of(0)
    ahead_ref[...] = distances(first_target, first_source, 0)
    lax.fori_loop(0, number, loop, 0)


def after(pair, *limits):
    return sum(jnp.where(pair >= limit, 1, 0) for limit in limits)


def local_pair(pair):
    target = after(pair, 3, 7, 11)
    source = pair - 3 * after(pair, 3) - 4 * after(pair, 7) - 3 * after(pair, 11)
    return target, source, source - target


def halo_pair(pair):
    target = pair - after(pair, 1, 5)
    source = (pair + 1) // 2
    return target, source, jnp.where(source < 2, source - 2, source + 2) - target


def local_kernel(mask_ref, points_ref, probes_ref, samples_ref, out_ref, targets_ref, sources_ref, high_ref, low_ref, ahead_ref):
    centred = (points_ref[...] - points_ref[:, 0:1]) * SCALE
    targets_ref[...] = features(centred, True).T.astype(bf16)
    sources_ref[...] = features(centred, False).astype(bf16)
    high, low = split2(probes_ref[...])
    high_ref[...] = high
    low_ref[...] = low
    out_ref[...] = samples_ref[...]
    near_blocks(targets_ref, sources_ref, high_ref, low_ref, ahead_ref, out_ref, mask_ref, 14, local_pair)


def shifted_gram(gram):
    row = lax.broadcasted_iota(jnp.int32, (KL, KL), 0)
    column = lax.broadcasted_iota(jnp.int32, (KL, KL), 1)
    diagonal = row == column
    trace = jnp.sum(jnp.where(diagonal, gram, 0.0))
    return gram + jnp.where(diagonal, SHIFT_RATIO * trace / KL + EPSILON, 0.0)


def inverse_factors(work_ref, panel_ref, number, beside=()):
    lane = lax.broadcasted_iota(jnp.int32, (number, KL), 1)
    wide_lane = lax.broadcasted_iota(jnp.int32, (KL, KL), 1)
    for first in range(0, KL, PANEL):
        rows = [work_ref[pl.ds(first + j, number, stride=KL), :] for j in range(PANEL)]
        entry = {
            (j, i): jnp.broadcast_to(rows[j][:, first + i : first + i + 1], (number, KL))
            for j in range(PANEL)
            for i in range(j, PANEL)
        }
        if first // PANEL < len(beside):
            beside[first // PANEL]()
        inside = (lane >= first) & (lane < first + PANEL)
        rows = [jnp.where(inside, jnp.where(lane == first + j, 1.0, 0.0), rows[j]) for j in range(PANEL)]
        for k in range(PANEL):
            scale = lax.rsqrt(entry[k, k])
            rows[k] = rows[k] * scale
            factor = {j: entry[k, j] * scale for j in range(k + 1, PANEL)}
            for j in range(k + 1, PANEL):
                for i in range(j, PANEL):
                    entry[j, i] = entry[j, i] - factor[j] * factor[i]
                rows[j] = rows[j] - factor[j] * rows[k]
            panel_ref[pl.ds(k, number, stride=PANEL), :] = rows[k]
        stop = first + PANEL
        for matrix in range(number):
            panel = panel_ref[matrix * PANEL : (matrix + 1) * PANEL, :]
            base = matrix * KL
            work_ref[base + first : base + stop, :] = jnp.where(
                wide_lane[:PANEL] < stop, panel, 0.0
            )
            if stop < KL:
                high, middle, low = split3(panel)
                left = jnp.concatenate([high, high, middle, middle, high, low], axis=0)
                right = jnp.concatenate([high, middle, high, middle, low, high], axis=0)
                update = fast(left, right, (0, 0))
                done = (wide_lane >= first) & (wide_lane < stop)
                old = jnp.where(done[stop:], 0.0, work_ref[base + stop : base + KL, :])
                work_ref[base + stop : base + KL, :] = old - update[stop:, :]


def halo_kernel(
    mask_ref, points_ref, partial_ref, probes_ref, before_ref, after_ref,
    basis_ref, coupling_ref, parent_ref, gram_ref,
    targets_ref, sources_ref, high_ref, low_ref, ahead_ref, remaining_ref, work_ref, panel_ref,
):
    size = 2 * LEAF
    centre = points_ref[:, 0:1]
    targets_ref[...] = features((points_ref[...] - centre) * SCALE, True).T.astype(bf16)
    for half, halo_ref in enumerate((before_ref, after_ref)):
        columns = slice(half * size, (half + 1) * size)
        parts = size // COLS
        halo_points = jnp.concatenate(
            [
                jnp.concatenate([halo_ref[size + d * parts + p : size + d * parts + p + 1, :] for p in range(parts)], axis=1)
                for d in range(3)
            ],
            axis=0,
        )
        sources_ref[:, columns] = features((halo_points - centre) * SCALE, False).astype(bf16)
        high, low = split2(halo_ref[:size, :])
        high_ref[columns, :] = high
        low_ref[columns, :] = low
    remaining_ref[...] = partial_ref[...]
    near_blocks(targets_ref, sources_ref, high_ref, low_ref, ahead_ref, remaining_ref, mask_ref, 6, halo_pair)

    leaves = range(COUNT)
    points_of = [slice(leaf * LEAF, (leaf + 1) * LEAF) for leaf in leaves]
    ranks_of = [slice(leaf * KL, (leaf + 1) * KL) for leaf in leaves]
    samples_products, probes_products = [], [None] * COUNT
    for leaf in leaves:
        rows = points_of[leaf]
        samples_products.append(dot(remaining_ref[rows, :KL], remaining_ref[rows, :], (0, 0)))
        work_ref[ranks_of[leaf], :] = shifted_gram(samples_products[leaf][:, :KL] / LEAF)

    def make_probes_product(leaf):
        rows = points_of[leaf]
        probes_products[leaf] = dot(remaining_ref[rows, :KL], probes_ref[rows, :], (0, 0))

    inverse_factors(work_ref, panel_ref, COUNT, [functools.partial(make_probes_product, leaf) for leaf in leaves])
    inverses = [work_ref[rows, :] for rows in ranks_of]
    reduced_probes, reduced_samples, crosses = [], [None] * COUNT, [None] * COUNT
    for leaf in leaves:
        reduced_probes.append(dot(inverses[leaf], probes_products[leaf], (1, 0)) / math.sqrt(LEAF))
        gram = dot(reduced_probes[leaf], reduced_probes[leaf], (1, 1)) / COLS
        work_ref[ranks_of[leaf], :] = shifted_gram(gram)

    def make_cross(leaf):
        reduced_samples[leaf] = dot(inverses[leaf], samples_products[leaf], (1, 0)) / LEAF
        crosses[leaf] = dot(reduced_samples[leaf], reduced_probes[leaf ^ 1], (1, 1)) / COLS

    def make_basis(leaf):
        rows = points_of[leaf]
        basis_ref[rows, :] = dot3(remaining_ref[rows, :KL], inverses[leaf], (1, 1)).astype(bf16)

    beside = [functools.partial(make, leaf) for make in (make_cross, make_basis) for leaf in leaves]
    inverse_factors(work_ref, panel_ref, COUNT, beside)
    for leaf in leaves:
        sibling = leaf ^ 1
        inverse = work_ref[ranks_of[sibling], :]
        coupling = dot(dot(crosses[leaf], inverse, (1, 1)), inverse, (1, 0))
        coupling_ref[ranks_of[leaf], :] = coupling.astype(bf16)
        parent_ref[ranks_of[leaf], :] = reduced_samples[leaf][:, :KL] - dot(
            coupling, reduced_probes[sibling][:, :KL], (1, 0)
        )
    gram_ref[...] = dot(parent_ref[...], parent_ref[...], (0, 0))


def parent_kernel(gram_ref, parent_ref, out_ref, work_ref, panel_ref):
    work_ref[...] = shifted_gram(gram_ref[...] / (LEAVES * KL))
    inverse_factors(work_ref, panel_ref, 1)
    out_ref[...] = dot3(parent_ref[...], work_ref[...], (1, 1))


def whole(memory_space=pltpu.VMEM):
    return pl.BlockSpec(memory_space=memory_space)


def exchange(block, axes):
    size = lax.axis_size(axes)
    return lax.all_to_all(jnp.broadcast_to(block, (size,) + block.shape), axes, 0, 0)


def total(block):
    near = ("x", "c")
    size = lax.axis_size(near)
    parts = lax.all_to_all(block.reshape(size, KL // size, KL), near, 0, 0).sum(0)
    parts = exchange(parts, "y").sum(0)
    parts = exchange(parts, "z").sum(0)
    return exchange(parts, near).reshape(KL, KL)


def shifted(block, distance):
    devices = range(lax.axis_size(AXES))
    route = [(i - distance, i) for i in devices if i - distance in devices]
    return lax.ppermute(block, AXES, route)


def packed(points, probes):
    rows = points.reshape(-1, COLS)
    return jnp.concatenate([probes, jnp.pad(rows, ((0, EXTRA - rows.shape[0]), (0, 0)))], axis=0)


def body(points, probes, samples, near_mask):
    size = COUNT * LEAF
    smem, vmem = whole(pltpu.SMEM), whole()
    params = pltpu.CompilerParams(vmem_limit_bytes=VMEM_LIMIT)
    up, down = (packed(points[:, part], probes[part]) for part in (slice(2 * LEAF, size), slice(0, 2 * LEAF)))
    before, after_block = shifted(up, 1), shifted(down, -1)
    near_scratch = [
        pltpu.VMEM((size, FEATURES), bf16),
        pltpu.VMEM((FEATURES, size), bf16),
        pltpu.VMEM((size, COLS), bf16),
        pltpu.VMEM((size, COLS), bf16),
        pltpu.VMEM((LEAF, HALF), f32),
    ]
    partial = pl.pallas_call(
        local_kernel,
        out_shape=jax.ShapeDtypeStruct((size, COLS), f32),
        in_specs=[smem, vmem, vmem, vmem],
        out_specs=vmem,
        scratch_shapes=near_scratch,
        compiler_params=params,
        cost_estimate=pl.CostEstimate(flops=14 * 8 * LEAF * LEAF * COLS, bytes_accessed=6 << 20, transcendentals=28 * LEAF * LEAF),
        name="local_blocks",
    )(near_mask, points, probes, samples)
    basis, coupling, parent_rows, gram = pl.pallas_call(
        halo_kernel,
        out_shape=[
            jax.ShapeDtypeStruct((size, KL), bf16),
            jax.ShapeDtypeStruct((COUNT * KL, KL), bf16),
            jax.ShapeDtypeStruct((COUNT * KL, KL), f32),
            jax.ShapeDtypeStruct((KL, KL), f32),
        ],
        in_specs=[smem] + [vmem] * 5,
        out_specs=[vmem] * 4,
        scratch_shapes=near_scratch + [
            pltpu.VMEM((size, COLS), f32),
            pltpu.VMEM((COUNT * KL, KL), f32),
            pltpu.VMEM((COUNT * PANEL, KL), f32),
        ],
        compiler_params=params,
        name="halo_blocks",
    )(near_mask, points, partial, probes, before, after_block)
    parent_basis = pl.pallas_call(
        parent_kernel,
        out_shape=jax.ShapeDtypeStruct((COUNT * KL, KL), f32),
        in_specs=[vmem, vmem],
        out_specs=vmem,
        scratch_shapes=[pltpu.VMEM((KL, KL), f32), pltpu.VMEM((PANEL, KL), f32)],
        compiler_params=params,
        name="parent",
    )(total(gram), parent_rows)
    return basis, coupling, parent_basis


def solution(mesh):
    fine = Mesh(mesh.devices.reshape(8, 4, 8, 2), AXES)
    return jax.shard_map(
        body,
        mesh=fine,
        in_specs=(P(None, AXES), P(AXES, None), P(AXES, None), P(AXES, None)),
        out_specs=(P(AXES, None), P(AXES, None), P(AXES, None)),
        check_vma=False,
    )
```

time: 122 us -> 105 us (0.86)
  Pallas kernels: 50 us -> 42.7 us
  blocking collectives: 54.1 us -> 48.8 us
  starting transfers between devices: 14.5 us -> 10.3 us
    all_to_all x1, blocking collectives: 18.9 us -> 7.94 us  [total(): lax.all_to_all(block.reshape(size, KL // size, KL), near, 0, 0).sum(0)]
    all_to_all x3, blocking collectives: 35.2 us -> 40.9 us  [exchange(): lax.all_to_all(jnp.broadcast_to(block, (size,) + block.shape), axes, 0, 0)]
    ppermute x4 -> x2, starting transfers between devices: 14.5 us -> 10.3 us  [shifted(): return lax.ppermute(block, AXES, route)]
    pallas_call x1, Pallas kernels: 27 us -> 23.1 us  [body(): pl.pallas_call(halo_kernel, out_shape=[jax.ShapeDtypeStruct((size, KL), b...]
    pallas_call x1, Pallas kernels: 17.7 us -> 14.3 us  [body(): pl.pallas_call(local_kernel, out_shape=jax.ShapeDtypeStruct((size, COLS),...]
  transfers between devices with their start and end apart: 4 -> 2, of which waited for: 0 -> 0; matrix products, arithmetic and copies ran while one was open for 0% -> 0% of each run, Pallas kernels for 15% -> 14%
where the time goes in v2:
time: 105 us
  blocking collectives  48.8 us (46%)
  Pallas kernels  42.7 us (41%)
  starting transfers between devices  10.3 us (10%)
  local copies, waits for them, and re-layouts  1.75 us (2%)
    all_to_all x3, blocking collectives, exchange(): lax.all_to_all(jnp.broadcast_to(block, (size,) + block.shape), axes, 0, 0)  40.9 us
    pallas_call x1, Pallas kernels, body(): pl.pallas_call(halo_kernel, out_shape=[jax.ShapeDtypeStruct((size, KL), b...  23.1 us
    pallas_call x1, Pallas kernels, body(): pl.pallas_call(local_kernel, out_shape=jax.ShapeDtypeStruct((size, COLS),...  14.3 us
    ppermute x2, starting transfers between devices, shifted(): return lax.ppermute(block, AXES, route)  10.3 us
    all_to_all x1, blocking collectives, total(): lax.all_to_all(block.reshape(size, KL // size, KL), near, 0, 0).sum(0)  7.94 us
    pallas_call x1, Pallas kernels, body(): pl.pallas_call(parent_kernel, out_shape=jax.ShapeDtypeStruct((COUNT * KL,...  5.26 us
  transfers between devices with their start and end apart: 2, of which 0 were waited for; matrix products, arithmetic and copies ran while one was open for 0% of the time, Pallas kernels for 14%

profile of v2, /device:TPU:1, one launch (start us, length us, event | category | flops | bytes accessed | tf_op | source)
XLA Modules:
  0.0 104.5 jit_solution(18264475770896077674)
XLA Ops:
  0.6 0.0 copy-start.1
  0.6 1.7 %fusion = (f32[1024,256]{1,0:T(8,128)S(1)}, f32[1024,256]{1,0:T(8,128)S(1)}) fusion(f32[2048,256]{1,0:T(8,128)} %probes_ref.3), kind=kLoop, calls=%fused_computation.3 | loop fusion | bytes 4194304 | tf_op jit(solution)/shard_map/slice | solution.py:303
  2.3 0.0 copy-done.1
  2.4 0.1 select_maximum_fusion.1
  2.4 4.6 %collective-permute-start = (f32[1040,256]{1,0:T(8,128)S(1)}, f32[1040,256]{1,0:T(8,128)S(1)}, u32[]{:S(2)}, u32[]{:S(2)}) collective-permute-start(f32[1040,256]{1,0:T(8,128)S(1)} %select_maximum_fusion.1), channel_id=1, source_target_pairs={{0,1},{1,2},{2,3},{3,4},{4,5},{5,6},{6,7},{7,8},{8,9},{9,10},{10,1... | collective-permute-start | bytes 3194888 | tf_op jit(solution)/shard_map/ppermute | solution.py:291
  7.1 0.0 copy-start
  7.1 0.0 copy-start.2
  7.1 0.1 select_maximum_fusion
  7.2 5.7 %collective-permute-start.1 = (f32[1040,256]{1,0:T(8,128)S(1)}, f32[1040,256]{1,0:T(8,128)S(1)}, u32[]{:S(2)}, u32[]{:S(2)}) collective-permute-start(f32[1040,256]{1,0:T(8,128)S(1)} %select_maximum_fusion), channel_id=1, source_target_pairs={{1,0},{2,1},{3,2},{4,3},{5,4},{6,5},{7,6},{8,7},{9,8},{10,9},{11,1... | collective-permute-start | bytes 3194888 | tf_op jit(solution)/shard_map/ppermute | solution.py:291
  12.9 0.0 copy-done
  12.9 0.0 copy-done.2
  12.9 14.3 %local_blocks.1.partial_ref = f32[2048,256]{1,0:T(8,128)S(1)} custom-call(s32[4,4]{1,0:T(4,128)S(1)} %copy-done.2, f32[3,2048]{1,0:T(4,128)S(1)} %copy-done.1, f32[2048,256]{1,0:T(8,128)S(1)} %copy-done, f32[2048,256]{1,0:T(8,128)} %samples_ref.1), custom_call_target="tpu_custom_call" | custom-call | flops 7516192768 | bytes 6291456 | tf_op jit(solution)/shard_map/local_blocks/pallas_call | solution.py:312
  27.2 0.0 collective-permute-done.before_ref
  27.2 0.0 collective-permute-done.1.after_ref
  27.2 23.1 %halo_blocks.1 = (bf16[2048,128]{1,0:T(8,128)(2,1)}, bf16[512,128]{1,0:T(8,128)(2,1)}, f32[512,128]{1,0:T(8,128)S(1)}, f32[128,128]{1,0:T(8,128)S(1)}) custom-call(s32[4,4]{1,0:T(4,128)S(1)} %copy-done.2, f32[3,2048]{1,0:T(4,128)S(1)} %copy-done.1, f32[2048,256]{1,0:T(8,128)S(1)} %local_blocks.1.partial_ref, f32[2048,256]{1,0:T(8,128)} %probes_ref.3, ...), custom_call_target="tpu_custom_call" | custom-call | tf_op jit(solution)/shard_map/halo_blocks/pallas_call | solution.py:322
  50.3 7.9 %all_to_all.20 = f32[8,16,128]{2,1,0:T(8,128)S(1)} all-to-all(f32[8,16,128]{2,1,0:T(8,128)S(1)} %bitcast.3), channel_id=1, replica_groups=mesh['z'=8,'x'=4,'y'=8,'c'=2] {'x','c'}, dimensions={0} | all-to-all | bytes 131072 | tf_op jit(solution)/shard_map/all_to_all | solution.py:282
  58.3 13.0 %all_to_all.21 = f32[8,16,128]{2,1,0:T(8,128)S(1)} all-to-all(f32[8,16,128]{2,1,0:T(8,128)S(1)} %broadcast_in_dim.9), channel_id=1, replica_groups=mesh['z'=8,'x'=4,'y'=8,'c'=2] {'y'}, dimensions={0} | all-to-all | bytes 131072 | tf_op jit(solution)/shard_map/all_to_all | solution.py:276
  71.3 17.0 %all_to_all.22 = f32[8,16,128]{2,1,0:T(8,128)S(1)} all-to-all(f32[8,16,128]{2,1,0:T(8,128)S(1)} %broadcast_in_dim.10), channel_id=1, replica_groups=mesh['z'=8,'x'=4,'y'=8,'c'=2] {'z'}, dimensions={0} | all-to-all | bytes 131072 | tf_op jit(solution)/shard_map/all_to_all | solution.py:276
  88.4 10.9 %all_to_all.23 = f32[8,16,128]{2,1,0:T(8,128)S(1)} all-to-all(f32[8,16,128]{2,1,0:T(8,128)S(1)} %broadcast_in_dim.11), channel_id=1, replica_groups=mesh['z'=8,'x'=4,'y'=8,'c'=2] {'x','c'}, dimensions={0} | all-to-all | bytes 131072 | tf_op jit(solution)/shard_map/all_to_all | solution.py:276
  99.2 5.3 %parent.1 = f32[512,128]{1,0:T(8,128)} custom-call(f32[128,128]{1,0:T(8,128)S(1)} %bitcast.2, f32[512,128]{1,0:T(8,128)S(1)} %get-tuple-element.10.parent_ref), custom_call_target="tpu_custom_call" | custom-call | tf_op jit(solution)/shard_map/parent/pallas_call | solution.py:340
  (9 shorter events, 0.1 us)
Async XLA Ops:
  0.6 1.7 %copy-start.1 = (f32[3,2048]{1,0:T(4,128)S(1)}, f32[3,2048]{1,0:T(4,128)}, u32[]{:S(2)}) copy-start(f32[3,2048]{1,0:T(4,128)} %points_ref.3) | copy-start | bytes 73732
  2.4 24.8 %collective-permute-start = (f32[1040,256]{1,0:T(8,128)S(1)}, f32[1040,256]{1,0:T(8,128)S(1)}, u32[]{:S(2)}, u32[]{:S(2)}) collective-permute-start(f32[1040,256]{1,0:T(8,128)S(1)} %select_maximum_fusion.1), channel_id=1, source_target_pairs={{0,1},{1,2},{2,3},{3,4},{4,5},{5,6},{6,7},{7,8},{8,9},{9,10},{10,1... | collective-permute-start | bytes 3194888 | tf_op jit(solution)/shard_map/ppermute | solution.py:291
  7.1 5.8 %copy-start = (f32[2048,256]{1,0:T(8,128)S(1)}, f32[2048,256]{1,0:T(8,128)}, u32[]{:S(2)}) copy-start(f32[2048,256]{1,0:T(8,128)} %probes_ref.3) | copy-start | bytes 6291460
  7.1 5.8 %copy-start.2 = (s32[4,4]{1,0:T(4,128)S(1)}, s32[4,4]{1,0:T(4,128)}, u32[]{:S(2)}) copy-start(s32[4,4]{1,0:T(4,128)} %mask_ref.3) | copy-start | bytes 196
  7.2 20.1 %collective-permute-start.1 = (f32[1040,256]{1,0:T(8,128)S(1)}, f32[1040,256]{1,0:T(8,128)S(1)}, u32[]{:S(2)}, u32[]{:S(2)}) collective-permute-start(f32[1040,256]{1,0:T(8,128)S(1)} %select_maximum_fusion), channel_id=1, source_target_pairs={{1,0},{2,1},{3,2},{4,3},{5,4},{6,5},{7,6},{8,7},{9,8},{10,9},{11,1... | collective-permute-start | bytes 3194888 | tf_op jit(solution)/shard_map/ppermute | solution.py:291
